TPU v7x, 128 devices: a whole 4x4x4 slice. The times are simulated.
128 devices in a mesh: dp: 16 (over y, x), row: 2 (over core), col: 4 (over z).
Axes of the slice: x: 4, y: 4, z: 4, core: 2. Of those that a mesh axis runs over, the one named last changes fastest.
Arguments:
- tokens: bfloat16 [16384, 8192], P(('dp', 'row'), 'col'), may hold values from -2200 to 2200, as said below
- gain: bfloat16 [8192], P('col'), may hold values from 0.5 to 1.5
- weight: bfloat16 [8192, 2048], P('col', 'row'), may hold values from -0.0625 to 0.0625
- d_out: bfloat16 [16384, 2048], P(('dp', 'col'), 'row'), may hold values from -6 to 6
- d_residual: bfloat16 [16384, 8192], P(('dp', 'row'), 'col'), may hold values from -1.5 to 1.5
Outputs:
- d_tokens: bfloat16 [16384, 8192], P(('dp', 'row'), 'col')
- d_weight: bfloat16 [8192, 2048], P(('col', 'dp'), 'row')
- d_gain: float32 [8192], P('col')
- d_log_scale: float32 [16384], P(('dp', 'row'))
Inputs may be any that keep to these rules, and one draw needn't show every extreme that they name: `tokens`: finite activations whose rows and features have differing scales.
All inputs are finite; a program needn't handle non-finite values.
Results may differ from a plain program's by a relative error of at most 0.017.
Values may be sent and summed in bfloat16 or wider, within the bound.
A program may use at most 64 MiB of HBM per device.

v0:
```python
import jax
import jax.numpy as jnp
from jax import lax
from jax.sharding import PartitionSpec as P

D = 8192
TOK_DEV = 512


def local(tokens, gain, weight, d_out, d_residual):
    tok_float = tokens.astype(jnp.float32)
    gain_float = gain.astype(jnp.float32)
    scale = float(TOK_DEV * lax.axis_size("row") * lax.axis_size("dp")) ** (-0.5)
    all_grads = lax.all_gather(d_out, "col", axis=0, tiled=True)
    local_squares = jnp.sum(tok_float * tok_float, axis=1)
    square_sum = lax.psum(local_squares, "col")
    inv_rms = lax.rsqrt(square_sum / D + 1e-05)[:, None]
    d_normed = lax.psum_scatter(
        lax.dot_general(
            all_grads, weight, (((1,), (1,)), ((), ())), preferred_element_type=jnp.float32
        ).astype(jnp.bfloat16),
        "row",
        scatter_dimension=0,
        tiled=True,
    ).astype(jnp.float32)
    scaled = d_normed * gain_float
    inner = lax.psum(jnp.sum(scaled * tok_float, axis=1), "col")[:, None]
    normed = (tok_float * inv_rms * gain_float).astype(jnp.bfloat16)
    partial_value = lax.dot_general(
        lax.all_gather(normed, "row", axis=0, tiled=True),
        all_grads,
        (((0,), (0,)), ((), ())),
        preferred_element_type=jnp.float32,
    )
    partial_rounded = partial_value.astype(jnp.bfloat16).astype(jnp.float32)
    summed = lax.psum(partial_rounded.astype(jnp.bfloat16), "dp").astype(jnp.float32)
    share_rows = partial_value.shape[0] // lax.axis_size("dp")
    own_rows = lax.dynamic_slice_in_dim(summed, lax.axis_index("dp") * share_rows, share_rows, 0)
    d_weight = (own_rows * scale).astype(jnp.bfloat16)
    local_gain = jnp.sum(d_normed * tok_float * inv_rms, axis=0)
    d_gain = lax.psum(local_gain, ("dp", "row")) * scale
    d_log_scale = (inner * inv_rms)[:, 0] * float(D) ** (-0.5)
    d_tokens = (
        d_residual.astype(jnp.float32)
        + inv_rms * scaled
        - tok_float * (inv_rms * inv_rms * inv_rms) * inner / D
    )
    return (d_tokens.astype(jnp.bfloat16), d_weight, d_gain, d_log_scale)


def solution(mesh):
    in_specs = (
        P(("dp", "row"), "col"),
        P("col"),
        P("col", "row"),
        P(("dp", "col"), "row"),
        P(("dp", "row"), "col"),
    )
    out_specs = (P(("dp", "row"), "col"), P(("col", "dp"), "row"), P("col"), P(("dp", "row")))
    return jax.shard_map(local, mesh=mesh, in_specs=in_specs, out_specs=out_specs, check_vma=False)
```

profile of v0, /device:TPU:0, one launch (start us, length us, event | category | flops | bytes accessed | tf_op | source)
XLA Modules:
  0.0 225.6 jit_solution(8201025934333962164)
XLA Ops:
  7.2 0.0 all-gather.3.cloned.1.call-start
  7.2 0.7 all-gather.3.cloned.1.call-update
  7.9 0.0 reduce-scatter.2.cloned.1.call-start
  7.9 35.3 %all-gather.3.cloned.1.call-done = bf16[1024,1024]{1,0:T(8,128)(2,1)} async-done(((bf16[256,1024]{1,0:T(8,128)(2,1)}), bf16[1024,1024]{1,0:T(8,128)(2,1)}) %all-gather.3.cloned.1.call-update) | async-done | bytes 2097168 | tf_op jit(solution)/shard_map/all_gather | solution.py:14
  43.2 9.3 %convolution_convert_fusion.1 = bf16[1024,2048]{1,0:T(8,128)(2,1)} fusion(bf16[1024,1024]{1,0:T(8,128)(2,1)} %all-gather.3.cloned.1.call-done, bf16[2048,1024]{1,0:T(8,128)(2,1)} %param.7), kind=kOutput, calls=%fused_computation.19 | convolution fusion | flops 4297064448 | bytes 10485760 | tf_op jit(solution)/shard_map/dot_general | solution.py:19
  52.5 0.0 copy-start.1
  52.5 0.0 copy-start
  52.5 0.0 reduce-scatter.2.cloned.1.call-update
  52.5 0.0 all-gather.5.cloned.1.call-start
  52.6 0.6 copy-done.1
  53.2 0.9 copy-done
  54.1 0.5 fusion.4
  54.6 8.5 %psum.28 = f32[512]{0:T(512)S(1)} all-reduce(f32[512]{0:T(512)S(1)} %fusion.4), channel_id=1, replica_groups=mesh['dp'=16,'row'=2,'col'=4] {'col'}, use_global_device_ids=true, to_apply=%region_1.0 | all-reduce | flops 512 | bytes 4096 | tf_op jit(solution)/shard_map/psum | solution.py:16
  63.1 4.3 %reduce-scatter.2.cloned.1.call-done = bf16[512,2048]{1,0:T(8,128)(2,1)} async-done(((bf16[1024,2048]{1,0:T(8,128)(2,1)}), bf16[512,2048]{1,0:T(8,128)(2,1)}) %reduce-scatter.2.cloned.1.call-update) | async-done | bytes 2097168 | tf_op jit(solution)/shard_map/reduce_scatter | solution.py:18
  67.4 3.2 %fusion.11 = (f32[2048]{0:T(1024)S(1)}, f32[512]{0:T(512)S(1)}) fusion(bf16[512,2048]{1,0:T(8,128)(2,1)S(1)} %copy-done, bf16[512,2048]{1,0:T(8,128)(2,1)} %reduce-scatter.2.cloned.1.call-done, f32[512]{0:T(512)S(1)} %add_rsqrt_fusion, f32[2048]{0:T(1024)S(1)} %convert_element_type.36), kind=kLoop, calls=%fused_computation.17 | loop fusion | flops 8386048 | bytes 4214784 | tf_op jit(solution)/shard_map/reduce_sum | solution.py:40
  70.6 10.8 %psum.29 = f32[512]{0:T(512)S(1)} all-reduce(f32[512]{0:T(512)S(1)} %get-tuple-element.5), channel_id=1, replica_groups=mesh['dp'=16,'row'=2,'col'=4] {'col'}, use_global_device_ids=true, to_apply=%region_4.0 | all-reduce | flops 512 | bytes 4096 | tf_op jit(solution)/shard_map/psum | solution.py:27
  81.3 0.6 multiply_multiply_fusion.1
  81.9 5.3 %fusion.9 = (bf16[512,2048]{1,0:T(8,128)(2,1)}, bf16[512,2048]{1,0:T(8,128)(2,1)}) fusion(bf16[512,2048]{1,0:T(8,128)(2,1)S(1)} %copy-done, f32[2048]{0:T(1024)S(1)} %convert_element_type.36, f32[512]{0:T(512)S(1)} %add_rsqrt_fusion, f32[512]{0:T(512)S(1)} %psum.29, f32[512]{0:T(512)S(1)} %get-tuple-element.9, ...), kind=kLoop, calls=%fused_computation.15 | loop fusion | flops 14680064 | bytes 10500096 | tf_op jit(solution)/shard_map/convert_element_type | solution.py:28
  87.3 0.0 all-gather.5.cloned.1.call-update
  87.3 0.0 all-reduce.2.cloned.1.call-start
  87.3 15.4 %all-gather.5.cloned.1.call-done = bf16[1024,2048]{1,0:T(8,128)(2,1)} async-done(((bf16[512,2048]{1,0:T(8,128)(2,1)}), bf16[1024,2048]{1,0:T(8,128)(2,1)}) %all-gather.5.cloned.1.call-update) | async-done | bytes 4194320 | tf_op jit(solution)/shard_map/all_gather | solution.py:30
  102.8 9.4 %convolution_convert_fusion = bf16[2048,1024]{1,0:T(8,128)(2,1)} fusion(bf16[1024,2048]{1,0:T(8,128)(2,1)} %all-gather.5.cloned.1.call-done, bf16[1024,1024]{1,0:T(8,128)(2,1)} %all-gather.3.cloned.1.call-done), kind=kOutput, calls=%fused_computation.18 | convolution fusion | flops 4297064448 | bytes 10485760 | tf_op jit(solution)/shard_map/dot_general | solution.py:29
  112.2 0.0 all-reduce.2.cloned.1.call-update
  112.2 69.8 %psum.31 = f32[2048]{0:T(1024)S(1)} all-reduce(f32[2048]{0:T(1024)S(1)} %get-tuple-element.4), channel_id=1, replica_groups=mesh['dp'=16,'row'=2,'col'=4] {'dp','row'}, use_global_device_ids=true, to_apply=%region_7.0 | all-reduce | flops 2048 | bytes 16384 | tf_op jit(solution)/shard_map/psum | solution.py:41
  182.0 0.6 broadcast_multiply_fusion
  182.6 34.8 %all-reduce.2.cloned.1.call-done = bf16[2048,1024]{1,0:T(8,128)(2,1)} async-done(((bf16[2048,1024]{1,0:T(8,128)(2,1)}), bf16[2048,1024]{1,0:T(8,128)(2,1)}) %all-reduce.2.cloned.1.call-update) | async-done | bytes 4194320 | tf_op jit(solution)/shard_map/psum | solution.py:36
  217.4 1.7 multiply_convert_fusion
  (2 shorter events, 0.0 us)
Async XLA Ops:
  7.2 36.1 %all-gather.3.cloned.1.call-start = ((), (), s32[]{:S(2)}) async-start(), calls=%async_computation.1 | async-start | bytes 2621440 | tf_op jit(solution)/shard_map/all_gather | solution.py:14
  7.9 59.5 %reduce-scatter.2.cloned.1.call-start = ((), (), s32[]{:S(2)}) async-start(), calls=%async_computation.2 | async-start | bytes 6291456 | tf_op jit(solution)/shard_map/reduce_scatter | solution.py:18
  52.5 0.7 copy-start.1
  52.5 1.6 copy-start
  52.5 50.3 %all-gather.5.cloned.1.call-start = ((), (), s32[]{:S(2)}) async-start(), calls=%async_computation.3 | async-start | bytes 6291456 | tf_op jit(solution)/shard_map/all_gather | solution.py:30
  87.3 130.1 %all-reduce.2.cloned.1.call-start = ((), (), s32[]{:S(2)}) async-start(), calls=%async_computation.4 | async-start | bytes 8388608 | tf_op jit(solution)/shard_map/psum | solution.py:36
Sparse Core Ops, SparseCore 0:
  9.7 33.5 all-gather.2
  52.7 14.6 reduce-scatter.1
  87.4 15.3 all-gather.4
  112.3 104.9 all-reduce.1
where the time goes:
time: 226 us
  waiting for transfers between devices  90.5 us (40%)
  blocking collectives  89 us (39%)
  matrix products  18.7 us (8%)
  between operations  13.8 us (6%)
  other arithmetic  11.9 us (5%)
    psum x1, blocking collectives, local(): d_gain = lax.psum(local_gain, ('dp', 'row')) * scale  69.8 us
    all_gather x1, waiting for transfers between devices, local(): all_grads = lax.all_gather(d_out, 'col', axis=0, tiled=True)  35.3 us
    psum x1, waiting for transfers between devices, local(): lax.psum(partial_rounded.astype(jnp.bfloat16), 'dp').astype(jnp.float32)  34.8 us
    all_gather x1, waiting for transfers between devices, local(): lax.all_gather(normed, 'row', axis=0, tiled=True)  15.4 us
    psum x1, blocking collectives, local(): inner = lax.psum(jnp.sum(scaled * tok_float, axis=1), 'col')[:, None]  10.8 us
    dot_general x1, matrix products, local(): lax.dot_general(lax.all_gather(normed, 'row', axis=0, tiled=True), all_gr...  9.41 us
    dot_general x1, matrix products, local(): lax.dot_general(all_grads, weight, (((1,), (1,)), ((), ())), preferred_el...  9.28 us
    psum x1, blocking collectives, local(): square_sum = lax.psum(local_squares, 'col')  8.5 us
  transfers between devices with their start and end apart: 4, of which 4 were waited for; matrix products, arithmetic and copies ran while one was open for 0% of the time, Pallas kernels for 0%

commit v1 on v0

v1 whole, which is shorter than its diff:
```python
import jax
import jax.numpy as jnp
from jax import lax
from jax.experimental import pallas as pl
from jax.experimental.pallas import tpu as pltpu
from jax.sharding import PartitionSpec as P

MESH = pl.DeviceIdType.MESH
BF16, F32 = jnp.bfloat16, jnp.float32
D = 8192
TOKENS = 16384
ROWS = 512
FEATS = 2048
COLS = 1024
QUARTER = 256
SIDE = 4
CHUNKS = ((0, 128), (128, 128), (256, 256), (512, 256), (768, 128), (896, 128))
N = len(CHUNKS)
PARTS = ((0, 512), (512, 512))


def dot(a, b, dims):
    return lax.dot_general(a, b, ((dims[:1], dims[1:]), ((), ())), preferred_element_type=F32)


def kernel(*refs):
    it = iter(refs)
    tok_hbm, gain_ref, w_hbm, dout_hbm, dres_hbm = [next(it) for _ in range(5)]
    dtok_hbm, dw_hbm, dgain_ref, dlog_ref = [next(it) for _ in range(4)]
    tok, tok_peer, grads, other, w, w_peer, dn, dres, scaled_t = [next(it) for _ in range(9)]
    lanes, sq, inv_row, inv_col, coef_col, inner_buf, dg_acc = [next(it) for _ in range(7)]
    dg_core, dg_x, dg_y, dw_t, dw_out = [next(it) for _ in range(5)]
    part, got1a, got1b, mid, got2a, got2b = [[next(it) for _ in range(N)] for _ in range(6)]
    local_sem, ag_s, ag_r, tp_s, tp_r, wp_s, wp_r, ot_s, ot_r = [next(it) for _ in range(9)]
    sq_s, sq_r, in_s, in_r, dgc_s, dgc_r, dgx_s, dgx_r, dgy_s, dgy_r = [next(it) for _ in range(10)]
    rs_s, rs_r, out_sem = [next(it) for _ in range(3)]

    dp, r, z = lax.axis_index("dp"), lax.axis_index("row"), lax.axis_index("col")
    y, x = dp // SIDE, dp % SIDE

    def dev(dy=0, dx=0, dr=0, dz=0):
        return ((y + dy) % SIDE * SIDE + (x + dx) % SIDE, (r + dr) % 2, (z + dz) % SIDE)

    sent = []

    def send(src, dst, ss, rs, to):
        c = pltpu.make_async_remote_copy(
            src_ref=src, dst_ref=dst, send_sem=ss, recv_sem=rs, device_id=to, device_id_type=MESH
        )
        c.start()
        sent.append(c)

    def arrived(dst, ss, rs):
        pltpu.make_async_remote_copy(
            src_ref=dst, dst_ref=dst, send_sem=ss, recv_sem=rs, device_id=dev(dr=1), device_id_type=MESH
        ).wait_recv()

    def load(src, dst, i):
        c = pltpu.make_async_copy(src, dst, local_sem.at[i])
        c.start()
        return c

    def slot(q):
        return pl.ds(pl.multiple_of((q + 2 * r) % SIDE * QUARTER, QUARTER), QUARTER)

    def half_slot(q, half):
        return pl.ds(pl.multiple_of((q + 2 * r) % SIDE * QUARTER + half * 128, 128), 128)

    tok_load = load(tok_hbm, tok, 0)
    own_load = load(dout_hbm, grads.at[slot(z)], 1)
    w_load = load(w_hbm, w, 2)
    res_load = load(dres_hbm, dres, 3)

    partners = [dev(dr=1)]
    partners += [dev(dz=d) for d in (1, 2, 3)] + [dev(dr=1, dz=d) for d in (1, 2, 3)]
    partners += [dev(dx=d) for d in (1, 2, 3)] + [dev(dy=d) for d in (1, 2, 3)]
    barrier = pltpu.get_barrier_semaphore()
    for partner in partners:
        pl.semaphore_signal(barrier, inc=1, device_id=partner, device_id_type=MESH)

    tok_load.wait()

    @pl.loop(0, ROWS // 16)
    def _(i):
        rows = pl.ds(pl.multiple_of(i * 16, 16), 16)
        acc = jnp.zeros((16, 128), F32)
        for j in range(FEATS // 128):
            t = tok[rows, pl.ds(j * 128, 128)].astype(F32)
            acc += t * t
        lanes[rows, :] = acc

    def lane_sums():
        total = jnp.sum(lanes[...].T, axis=0, keepdims=True)
        return jnp.broadcast_to(total, (8, ROWS))

    sq[0, z] = lane_sums()
    pl.semaphore_wait(barrier, len(partners))

    def columns(k):
        return pl.ds(CHUNKS[k][0], CHUNKS[k][1])

    def gather_send(k):
        src = dout_hbm.at[:, columns(k)]
        dst = grads.at[slot(z), columns(k)]
        send(src, dst, ag_s.at[k, 0], ag_r.at[k, 0], dev(dz=1))
        send(src, dst, ag_s.at[k, 1], ag_r.at[k, 1], dev(dz=3))
        if k == 0:
            send(src, dst, ag_s.at[k, 2], ag_r.at[k, 2], dev(dz=2))

    def gather_relay(k):
        if k == 0:
            return
        low, high = grads.at[half_slot(z + 1, 0), columns(k)], grads.at[half_slot(z + 3, 1), columns(k)]
        arrived(grads.at[slot(z + 3), columns(k)], ag_s.at[k, 0], ag_r.at[k, 0])
        send(high, high, ag_s.at[k, 3], ag_r.at[k, 3], dev(dz=1))
        arrived(grads.at[slot(z + 1), columns(k)], ag_s.at[k, 1], ag_r.at[k, 1])
        send(low, low, ag_s.at[k, 2], ag_r.at[k, 2], dev(dz=3))

    def gather_wait(k):
        if k == 0:
            for j, d in ((0, 3), (1, 1), (2, 2)):
                arrived(grads.at[slot(z + d), columns(k)], ag_s.at[k, j], ag_r.at[k, j])
            own_load.wait()
        else:
            arrived(grads.at[half_slot(z + 2, 0), columns(k)], ag_s.at[k, 2], ag_r.at[k, 2])
            arrived(grads.at[half_slot(z + 2, 1), columns(k)], ag_s.at[k, 3], ag_r.at[k, 3])
        send(
            grads.at[pl.ds(ROWS, ROWS), columns(k)], other.at[:, columns(k)], ot_s.at[k], ot_r.at[k], dev(dr=1)
        )

    send(sq.at[0, z], sq.at[1, z], sq_s.at[0], sq_r.at[1, z], dev(dr=1))
    for d in (1, 2, 3):
        send(sq.at[0, z], sq.at[0, z], sq_s.at[d], sq_r.at[0, z], dev(dz=d))
        send(sq.at[0, z], sq.at[1, z], sq_s.at[3 + d], sq_r.at[1, z], dev(dr=1, dz=d))
    gather_send(0)
    for b in range(SIDE):
        cols = pl.ds(b * 512, 512)
        send(tok_hbm.at[:, cols], tok_peer.at[:, cols], tp_s.at[b], tp_r.at[b], dev(dr=1))
    gather_send(1)
    gather_send(2)
    for b in range(SIDE):
        rows = pl.ds(b * 512, 512)
        send(w_hbm.at[rows], w_peer.at[rows], wp_s.at[b], wp_r.at[b], dev(dr=1))

    for d in (1, 2, 3):
        q = (z + d) % SIDE
        arrived(sq.at[0, q], sq_s.at[0], sq_r.at[0, q])
    for q in range(SIDE):
        arrived(sq.at[1, q], sq_s.at[0], sq_r.at[1, q])
    for side in range(2):
        total = sq[side, 0] + sq[side, 1] + sq[side, 2] + sq[side, 3]
        inv_row[:, pl.ds(side * ROWS, ROWS)] = lax.rsqrt(total * (1.0 / D) + 1e-05)

    def as_column(row):
        return jnp.broadcast_to(row[0:1], (128, ROWS)).T

    inv_col[...] = as_column(inv_row[:, 0:ROWS])

    def product(k):
        start, width = CHUNKS[k]
        cq = width // 4
        for s in range(SIDE):
            toks = pl.ds(s * QUARTER, QUARTER)
            g = grads[toks, pl.ds(start, width)].T.astype(F32)
            scaled_t[pl.ds(0, width), toks] = (g * inv_row[0:1, toks]).astype(BF16)

        def block(b):
            feats = pl.ds(b * 512, 512) if isinstance(b, int) else pl.ds(pl.multiple_of(b * 512, 512), 512)
            res = dot(scaled_t[pl.ds(0, width), pl.ds(0, ROWS)], tok[:, feats], (1, 0))
            res += dot(scaled_t[pl.ds(0, width), pl.ds(ROWS, ROWS)], tok_peer[:, feats], (1, 0))
            res = res.astype(BF16)
            for j in range(SIDE):
                for h in range(2):
                    for u in range(2):
                        lo = (2 * h + u) * cq
                        piece = res[lo : lo + cq, j * 128 : j * 128 + 128]
                        if h == 0:
                            part[k][h, u, j, b] = piece
                        else:
                            part[k][h, u, b, j] = piece

        if k == 0:
            for b in range(SIDE):
                cols = pl.ds(b * 512, 512)
                arrived(tok_peer.at[:, cols], tp_s.at[b], tp_r.at[b])
                block(b)
        else:
            pl.loop(0, SIDE)(block)

    def axis(h, stage):
        if (h == 0) == (stage == 0):
            return x, (lambda d: dev(dx=d))
        return y, (lambda d: dev(dy=d))

    def reduce_start(k, stage):
        src, got_a, got_b = (part, got1a, got1b) if stage == 0 else (mid, got2a, got2b)
        for h in range(2):
            m, to = axis(h, stage)
            ss, rs = rs_s.at[k, stage, h], rs_r.at[k, stage, h]
            far, up, down = (m + 2) % SIDE, (m + 1) % SIDE, (m + 3) % SIDE
            send(src[k].at[h, 0, far], got_a[k].at[h, 0], ss.at[0], rs.at[0], to(1))
            send(src[k].at[h, 1, far], got_a[k].at[h, 1], ss.at[1], rs.at[1], to(3))
            send(src[k].at[h, 1, up], got_b[k].at[h, 0, 1], ss.at[2], rs.at[2], to(1))
            send(src[k].at[h, 0, down], got_b[k].at[h, 1, 0], ss.at[3], rs.at[3], to(3))

    def add(a, b):
        return (a.astype(F32) + b.astype(F32)).astype(BF16)

    def reduce_pass(k, stage):
        src, got_a, got_b = (part, got1a, got1b) if stage == 0 else (mid, got2a, got2b)
        for h in range(2):
            m, to = axis(h, stage)
            ss, rs = rs_s.at[k, stage, h], rs_r.at[k, stage, h]
            up, down = (m + 1) % SIDE, (m + 3) % SIDE
            arrived(got_a[k].at[h, 0], ss.at[0], rs.at[0])
            src[k][h, 0, up] = add(src[k][h, 0, up], got_a[k][h, 0])
            send(src[k].at[h, 0, up], got_b[k].at[h, 0, 0], ss.at[4], rs.at[4], to(1))
            arrived(got_a[k].at[h, 1], ss.at[1], rs.at[1])
            src[k][h, 1, down] = add(src[k][h, 1, down], got_a[k][h, 1])
            send(src[k].at[h, 1, down], got_b[k].at[h, 1, 1], ss.at[5], rs.at[5], to(3))

    def reduce_end(k, stage):
        src, got_b = (part, got1b) if stage == 0 else (mid, got2b)
        cq = CHUNKS[k][1] // 4
        for h in range(2):
            m, _ = axis(h, stage)
            ss, rs = rs_s.at[k, stage, h], rs_r.at[k, stage, h]
            arrived(got_b[k].at[h, 0, 1], ss.at[2], rs.at[2])
            arrived(got_b[k].at[h, 1, 0], ss.at[3], rs.at[3])
            arrived(got_b[k].at[h, 0, 0], ss.at[4], rs.at[4])
            arrived(got_b[k].at[h, 1, 1], ss.at[5], rs.at[5])
            for u in range(2):
                total = src[k][h, u, m].astype(F32)
                total += got_b[k][h, 0, u].astype(F32)
                total += got_b[k][h, 1, u].astype(F32)
                if stage == 0:
                    mid[k][h, u] = total.astype(BF16)
                else:
                    dw_t[pl.ds((2 * h + u) * cq, cq), :] = total

    def finish(k):
        start, width = CHUNKS[k]
        own = gain_ref[0:1, pl.ds(pl.multiple_of(dp * 128, 128), 128)].astype(F32) * float(TOKENS) ** (-0.5)
        dw_out[:, pl.ds(start, width)] = (dw_t[pl.ds(0, width), :] * own).T.astype(BF16)

    def normed_grad(p):
        cols = pl.ds(*PARTS[p])
        for k in range(N):
            if PARTS[p][0] <= CHUNKS[k][0] < PARTS[p][0] + PARTS[p][1]:
                arrived(other.at[:, columns(k)], ot_s.at[k], ot_r.at[k])
        if p == 0:
            w_load.wait()
            for b in range(SIDE):
                arrived(w_peer.at[pl.ds(b * 512, 512)], wp_s.at[b], wp_r.at[b])

        @pl.loop(0, SIDE)
        def _(b):
            feats = pl.ds(pl.multiple_of(b * 512, 512), 512)
            res = dot(grads[pl.ds(0, ROWS), cols], w[feats, cols], (1, 1))
            res += dot(other[:, cols], w_peer[feats, cols], (1, 1))
            if p == 0:
                dn[:, feats] = res
            else:
                dn[:, feats] += res

    def inner_start():
        dg_acc[...] = jnp.zeros_like(dg_acc)

        @pl.loop(0, ROWS // 16)
        def _(i):
            rows = pl.ds(pl.multiple_of(i * 16, 16), 16)
            inv = inv_col[rows, :]
            acc = jnp.zeros((16, 128), F32)
            for j in range(FEATS // 128):
                cols = pl.ds(j * 128, 128)
                prod = dn[rows, cols] * tok[rows, cols].astype(F32)
                acc += prod * gain_ref[0:1, cols].astype(F32)
                prod = prod * inv
                dg_acc[:, cols] += prod[0:8] + prod[8:16]
            lanes[rows, :] = acc

        inner_buf[z] = lane_sums()
        for d in (1, 2, 3):
            send(inner_buf.at[z], inner_buf.at[z], in_s.at[d], in_r.at[z], dev(dz=d))
        for j in range(FEATS // 128):
            dg_core[r, pl.ds(j, 1), :] = jnp.sum(dg_acc[:, pl.ds(j * 128, 128)], axis=0, keepdims=True)
        send(dg_core.at[r], dg_core.at[r], dgc_s, dgc_r, dev(dr=1))

    def gain_x():
        arrived(dg_core.at[1 - r], dgc_s, dgc_r)
        dg_x[x] = dg_core[0] + dg_core[1]
        for d in (1, 2, 3):
            send(dg_x.at[x], dg_x.at[x], dgx_s.at[d], dgx_r.at[x], dev(dx=d))

    def gain_y():
        for d in (1, 2, 3):
            q = (x + d) % SIDE
            arrived(dg_x.at[q], dgx_s.at[0], dgx_r.at[q])
        dg_y[y] = dg_x[0] + dg_x[1] + dg_x[2] + dg_x[3]
        for d in (1, 2, 3):
            send(dg_y.at[y], dg_y.at[y], dgy_s.at[d], dgy_r.at[y], dev(dy=d))

    def gain_end():
        for d in (1, 2, 3):
            q = (y + d) % SIDE
            arrived(dg_y.at[q], dgy_s.at[0], dgy_r.at[q])
        dgain_ref[...] = (dg_y[0] + dg_y[1] + dg_y[2] + dg_y[3]) * float(TOKENS) ** (-0.5)

    writes = []

    def write(src, dst, i):
        c = pltpu.make_async_copy(src, dst, out_sem.at[i])
        c.start()
        writes.append(c)

    def tokens_end():
        for d in (1, 2, 3):
            q = (z + d) % SIDE
            arrived(inner_buf.at[q], in_s.at[0], in_r.at[q])
        inner = inner_buf[0] + inner_buf[1] + inner_buf[2] + inner_buf[3]
        inv = inv_row[:, 0:ROWS]
        log_scale = inner * inv * float(D) ** (-0.5)
        for j in range(SIDE):
            dlog_ref[pl.ds(j, 1), :] = log_scale[0:1, j * 128 : j * 128 + 128]
        coef_col[...] = as_column(inv * inv * inv * inner * (1.0 / D))
        res_load.wait()
        for q in range(SIDE):

            @pl.loop(0, 8)
            def _(i):
                rows = pl.ds(pl.multiple_of(q * 128 + i * 16, 16), 16)
                inv_c, coef = inv_col[rows, :], coef_col[rows, :]
                for j in range(FEATS // 128):
                    cols = pl.ds(j * 128, 128)
                    scaled = dn[rows, cols] * gain_ref[0:1, cols].astype(F32)
                    value = dres[rows, cols].astype(F32) + inv_c * scaled
                    dres[rows, cols] = (value - tok[rows, cols].astype(F32) * coef).astype(BF16)

            rows = pl.ds(q * 128, 128)
            write(dres.at[rows], dtok_hbm.at[rows], q)

    for i in range(N + 4):
        if 1 <= i and i + 1 < N:
            gather_relay(i + 1)
            if i + 2 < N:
                gather_send(i + 2)
        if i < N:
            gather_wait(i)
            product(i)
            reduce_start(i, 0)
        if i == 0:
            gather_relay(1)
        if 0 <= i - 1 < N:
            reduce_pass(i - 1, 0)
        if 0 <= i - 2 < N:
            reduce_end(i - 2, 0)
            reduce_start(i - 2, 1)
        if 0 <= i - 3 < N:
            reduce_pass(i - 3, 1)
        if 0 <= i - 4 < N:
            reduce_end(i - 4, 1)
            finish(i - 4)
        if i == 4:
            normed_grad(0)
        if i == N:
            normed_grad(1)
            inner_start()
        if i == N + 1:
            gain_x()
            tokens_end()
        if i == N + 2:
            gain_y()
    write(dw_out, dw_hbm, 4)
    gain_end()
    for c in sent:
        c.wait_send()
    for c in writes:
        c.wait()


def local(tokens, gain, weight, d_out, d_residual):
    vmem, dma = pltpu.VMEM, pltpu.SemaphoreType.DMA
    cqs = [width // 4 for _, width in CHUNKS]
    scratch = [
        vmem((ROWS, FEATS), BF16),
        vmem((ROWS, FEATS), BF16),
        vmem((2 * ROWS, COLS), BF16),
        vmem((ROWS, COLS), BF16),
        vmem((FEATS, COLS), BF16),
        vmem((FEATS, COLS), BF16),
        vmem((ROWS, FEATS), F32),
        vmem((ROWS, FEATS), BF16),
        vmem((256, 2 * ROWS), BF16),
        vmem((ROWS, 128), F32),
        vmem((2, SIDE, 8, ROWS), F32),
        vmem((8, 2 * ROWS), F32),
        vmem((ROWS, 128), F32),
        vmem((ROWS, 128), F32),
        vmem((SIDE, 8, ROWS), F32),
        vmem((8, FEATS), F32),
        vmem((2, 16, 128), F32),
        vmem((SIDE, 16, 128), F32),
        vmem((SIDE, 16, 128), F32),
        vmem((256, 128), F32),
        vmem((128, COLS), BF16),
    ]
    scratch += [vmem((2, 2, SIDE, SIDE, c, 128), BF16) for c in cqs]
    scratch += [vmem((2, 2, SIDE, c, 128), BF16) for c in cqs]
    scratch += [vmem((2, 2, 2, SIDE, c, 128), BF16) for c in cqs]
    scratch += [vmem((2, 2, SIDE, c, 128), BF16) for c in cqs]
    scratch += [vmem((2, 2, c, 128), BF16) for c in cqs]
    scratch += [vmem((2, 2, 2, c, 128), BF16) for c in cqs]
    scratch += [
        dma((4,)),
        dma((N, 4)),
        dma((N, 4)),
        dma((4,)),
        dma((4,)),
        dma((4,)),
        dma((4,)),
        dma((N,)),
        dma((N,)),
        dma((7,)),
        dma((2, SIDE)),
        dma((4,)),
        dma((SIDE,)),
        dma,
        dma,
        dma((4,)),
        dma((SIDE,)),
        dma((4,)),
        dma((SIDE,)),
        dma((N, 2, 2, 6)),
        dma((N, 2, 2, 6)),
        dma((5,)),
    ]
    hbm, in_vmem = pl.BlockSpec(memory_space=pl.ANY), pl.BlockSpec(memory_space=pltpu.VMEM)
    d_tokens, d_weight, d_gain, d_log = pl.pallas_call(
        kernel,
        name="fused",
        out_shape=(
            jax.ShapeDtypeStruct((ROWS, FEATS), BF16),
            jax.ShapeDtypeStruct((128, COLS), BF16),
            jax.ShapeDtypeStruct((16, 128), F32),
            jax.ShapeDtypeStruct((4, 128), F32),
        ),
        in_specs=[hbm, in_vmem, hbm, hbm, hbm],
        out_specs=(hbm, hbm, in_vmem, in_vmem),
        scratch_shapes=scratch,
        compiler_params=pltpu.CompilerParams(
            collective_id=0, has_side_effects=True, vmem_limit_bytes=60 * 2**20
        ),
        cost_estimate=pl.CostEstimate(flops=8 * 2**30, bytes_accessed=12 * 2**20, transcendentals=0),
    )(tokens, gain.reshape(1, FEATS), weight, d_out, d_residual)
    return d_tokens, d_weight, d_gain.reshape(FEATS), d_log.reshape(ROWS)


def solution(mesh):
    in_specs = (
        P(("dp", "row"), "col"),
        P("col"),
        P("col", "row"),
        P(("dp", "col"), "row"),
        P(("dp", "row"), "col"),
    )
    out_specs = (P(("dp", "row"), "col"), P(("col", "dp"), "row"), P("col"), P(("dp", "row")))
    return jax.shard_map(local, mesh=mesh, in_specs=in_specs, out_specs=out_specs, check_vma=False)
```

time: 226 us -> 73 us (0.32)
  waiting for transfers between devices: 90.5 us -> 0 us
  blocking collectives: 89 us -> 0 us
  Pallas kernels: 0 us -> 65.8 us
  matrix products: 18.7 us -> 0 us
  between operations: 13.8 us -> 0.67 us
  other arithmetic: 11.9 us -> 0 us
  local copies, waits for them, and re-layouts: 1.53 us -> 6.38 us
    psum x3 -> x0, blocking collectives: 89 us -> none  [the longest x1 69.8 us: local(): d_gain = lax.psum(local_gain, ('dp', 'row')) * scale]
    pallas_call x0 -> x1, Pallas kernels: none -> 65.8 us  [local(): pl.pallas_call(kernel, name='fused', out_shape=(jax.ShapeDtypeStruct((ROW...]
    all_gather x2 -> x0, waiting for transfers between devices: 50.7 us -> none  [the longest x1 35.3 us: local(): all_grads = lax.all_gather(d_out, 'col', axis=0, tiled=True)]
    psum x1 -> x0, waiting for transfers between devices: 34.8 us -> none  [local(): lax.psum(partial_rounded.astype(jnp.bfloat16), 'dp').astype(jnp.float32)]
    dot_general x2 -> x0, matrix products: 18.7 us -> none  [the longest x1 9.41 us: local(): lax.dot_general(lax.all_gather(normed, 'row', axis=0, tiled=True), all_gr...]
    convert_element_type x3 -> x0, other arithmetic: 7.06 us -> none  [the longest x1 5.35 us: local(): normed = (tok_float * inv_rms * gain_float).astype(jnp.bfloat16)]
    reduce_scatter x1 -> x0, waiting for transfers between devices: 4.29 us -> none  [local(): lax.psum_scatter(lax.dot_general(all_grads, weight, (((1,), (1,)), ((), (...]
    reduce_sum x2 -> x0, other arithmetic: 3.66 us -> none  [the longest x1 3.18 us: local(): local_gain = jnp.sum(d_normed * tok_float * inv_rms, axis=0)]
  transfers between devices with their start and end apart: 4 -> 0, of which waited for: 4 -> 0; matrix products, arithmetic and copies ran while one was open for 0% -> 0% of each run, Pallas kernels for 0% -> 0%
where the time goes in v1:
time: 73 us; the launch traced here: 72.8 us
  Pallas kernels  65.8 us (90%)
  local copies, waits for them, and re-layouts  6.38 us (9%)
    pallas_call x1, Pallas kernels, local(): pl.pallas_call(kernel, name='fused', out_shape=(jax.ShapeDtypeStruct((ROW...  65.8 us
    unnamed x10, local copies, waits for them, and re-layouts  5.09 us

profile of v1, /device:TPU:0, one launch (start us, length us, event | category | flops | bytes accessed | tf_op | source)
XLA Modules:
  0.0 72.8 jit_solution(15601527887124521067)
XLA Ops:
  0.6 1.3 %reshape.17.refs_1_ = bf16[1,2048]{1,0:T(2,128)(2,1)} reshape(bf16[2048]{0:T(1024)(128)(2,1)} %param.6) | data formatting | bytes 8192 | tf_op jit(solution)/shard_map/reshape | solution.py:454
  1.9 65.8 %fused.1 = (bf16[512,2048]{1,0:T(8,128)(2,1)}, bf16[128,1024]{1,0:T(8,128)(2,1)}, f32[16,128]{1,0:T(8,128)}, f32[4,128]{1,0:T(4,128)}) custom-call(bf16[512,2048]{1,0:T(8,128)(2,1)} %refs_0_.1, bf16[1,2048]{1,0:T(2,128)(2,1)} %reshape.17.refs_1_, bf16[2048,1024]{1,0:T(8,128)(2,1)} %refs_2_.1, bf16[256,1024]{1,0:T(8,128)(2,1)} %refs_3_.1, ...), custom_call_target="tpu_custom_call" | custom-call | flops 8589934592 | bytes 12582912 | tf_op jit(solution)/shard_map/fused/pallas_call | solution.py:438
  67.7 0.0 copy-start
  67.7 0.0 copy-start.1
  67.7 0.0 copy-start.2
  67.7 3.2 %copy.13 = bf16[512,2048]{1,0:T(8,128)(2,1)} copy(bf16[512,2048]{1,0:T(8,128)(2,1)} %get-tuple-element.16) | data formatting | bytes 4194304
  70.9 0.0 copy-done
  70.9 0.7 copy.14
  71.6 0.0 copy-done.1
  71.6 0.6 copy.15
  72.2 0.0 copy-done.2
  72.2 0.6 copy.16
Async XLA Ops:
  67.7 3.2 %copy-start = (bf16[128,1024]{1,0:T(8,128)(2,1)S(1)}, bf16[128,1024]{1,0:T(8,128)(2,1)}, u32[]{:S(2)}) copy-start(bf16[128,1024]{1,0:T(8,128)(2,1)} %get-tuple-element.17) | copy-start | bytes 786436
  67.7 3.9 %copy-start.1 = (f32[16,128]{1,0:T(8,128)S(1)}, f32[16,128]{1,0:T(8,128)}, u32[]{:S(2)}) copy-start(f32[16,128]{1,0:T(8,128)} %get-tuple-element.10) | copy-start | bytes 24580
  67.7 4.5 %copy-start.2 = (f32[4,128]{1,0:T(4,128)S(1)}, f32[4,128]{1,0:T(4,128)}, u32[]{:S(2)}) copy-start(f32[4,128]{1,0:T(4,128)} %get-tuple-element.11) | copy-start | bytes 6148

commit v2 on v1

v2 whole, which is shorter than its diff:
```python
import jax
import jax.numpy as jnp
from jax import lax
from jax.experimental import pallas as pl
from jax.experimental.pallas import tpu as pltpu
from jax.sharding import PartitionSpec as P

MESH = pl.DeviceIdType.MESH
BF16, F32 = jnp.bfloat16, jnp.float32
D = 8192
TOKENS = 16384
ROWS = 512
FEATS = 2048
COLS = 1024
QUARTER = 256
SIDE = 4
SLABS = 8
CHUNKS = ((0, 1), (1, 1), (2, 2), (4, 2), (6, 1), (7, 1))
N = len(CHUNKS)
STRAIGHT = ((0, 0), (0, 0), (0, 0), (0, 0), (0, 1), (1, 1))
PARTS = (((0, 4), (0, 4)), ((4, 8), (4, 8)))


def dot(a, b, dims):
    return lax.dot_general(a, b, ((dims[:1], dims[1:]), ((), ())), preferred_element_type=F32)


def kernel(*refs):
    it = iter(refs)
    tok_hbm, gain_hbm, w_hbm, dout_hbm, dres_hbm = [next(it) for _ in range(5)]
    dtok_ref, dw_ref, dgain_ref, dlog_ref = [next(it) for _ in range(4)]
    tok, tok_peer, grads, other, w, w_peer, dn, dres, scaled_t = [next(it) for _ in range(9)]
    gain_flat, gain_row, lanes, sq, inv_row, inv_col, coef_col, inner_buf = [next(it) for _ in range(8)]
    dg_acc, dg_a, dg_b, dw_t = [next(it) for _ in range(4)]
    part, got1a, got1b, mid, got2a, got2b = [[next(it) for _ in range(N)] for _ in range(6)]
    local_sem, ag_s, ag_r, tp_s, tp_r, wp_s, wp_r, ot_s, ot_r = [next(it) for _ in range(9)]
    sq_s, sq_r, in_s, in_r, ga_s, ga_r, gb_s, gb_r, rs_s, rs_r = [next(it) for _ in range(10)]

    dp, r, z = lax.axis_index("dp"), lax.axis_index("row"), lax.axis_index("col")
    y, x = dp // SIDE, dp % SIDE

    def dev(dy=0, dx=0, dr=0, dz=0):
        return ((y + dy) % SIDE * SIDE + (x + dx) % SIDE, (r + dr) % 2, (z + dz) % SIDE)

    def send(src, dst, ss, rs, to):
        pltpu.make_async_remote_copy(
            src_ref=src, dst_ref=dst, send_sem=ss, recv_sem=rs, device_id=to, device_id_type=MESH
        ).start()

    def descriptor(ref, sem):
        return pltpu.make_async_remote_copy(
            src_ref=ref, dst_ref=ref, send_sem=sem, recv_sem=sem, device_id=dev(dr=1), device_id_type=MESH
        )

    def arrived(ref, sem):
        descriptor(ref, sem).wait_recv()

    def left(ref, sem):
        descriptor(ref, sem).wait_send()

    def load(src, dst, i):
        c = pltpu.make_async_copy(src, dst, local_sem.at[i])
        c.start()
        return c

    def slot(q):
        return pl.ds(pl.multiple_of((q + 2 * r) % SIDE * QUARTER, QUARTER), QUARTER)

    def half_slot(q, half):
        return pl.ds(pl.multiple_of((q + 2 * r) % SIDE * QUARTER + half * 128, 128), 128)

    def slabs(k):
        return pl.ds(*CHUNKS[k])

    partners = [dev(dr=1)]
    partners += [dev(dz=d) for d in (1, 2, 3)] + [dev(dr=1, dz=d) for d in (1, 2, 3)]
    partners += [dev(dx=d) for d in (1, 2, 3)] + [dev(dr=1, dx=d) for d in (1, 2, 3)]
    partners += [dev(dy=d) for d in (1, 2, 3)]
    barrier = pltpu.get_barrier_semaphore()
    for partner in partners:
        pl.semaphore_signal(barrier, inc=1, device_id=partner, device_id_type=MESH)

    tok_load = load(tok_hbm, tok, 0)
    for c in range(SLABS):
        load(dout_hbm.at[:, pl.ds(c * 128, 128)], grads.at[c, slot(z)], 1)
    gain_load = load(gain_hbm, gain_flat, 2)
    w_load = load(w_hbm, w, 3)
    res_load = load(dres_hbm, dres, 4)

    tok_load.wait()

    @pl.loop(0, ROWS // 16)
    def _(i):
        rows = pl.ds(pl.multiple_of(i * 16, 16), 16)
        acc = jnp.zeros((16, 128), F32)
        for j in range(FEATS // 128):
            t = tok[rows, pl.ds(j * 128, 128)].astype(F32)
            acc += t * t
        lanes[rows, :] = acc

    def lane_sums():
        total = jnp.sum(lanes[...].T, axis=0, keepdims=True)
        return jnp.broadcast_to(total, (8, ROWS))

    own_sq = sq.at[z]
    own_sq[...] = lane_sums()
    own_quarter = grads.at[:, slot(z)]
    pltpu.make_async_copy(own_quarter, own_quarter, local_sem.at[1]).wait()
    pl.semaphore_wait(barrier, len(partners))

    def gather_send(k):
        own = grads.at[slabs(k), slot(z)]
        for d in (1, 3) if k else (1, 3, 2):
            send(own, own, ag_s, ag_r.at[k, 0], dev(dz=d))

    def gather_relay(k):
        if k == 0:
            return
        arrived(grads.at[slabs(k), pl.ds(0, 2 * QUARTER)], ag_r.at[k, 0])
        low, high = grads.at[slabs(k), half_slot(z + 1, 0)], grads.at[slabs(k), half_slot(z + 3, 1)]
        send(low, low, ag_s, ag_r.at[k, 1], dev(dz=3))
        send(high, high, ag_s, ag_r.at[k, 1], dev(dz=1))

    def gather_wait(k):
        if k == 0:
            arrived(grads.at[slabs(k), pl.ds(0, 3 * QUARTER)], ag_r.at[k, 0])
        else:
            arrived(grads.at[slabs(k), pl.ds(0, QUARTER)], ag_r.at[k, 1])
        send(grads.at[slabs(k), pl.ds(ROWS, ROWS)], other.at[slabs(k)], ot_s, ot_r.at[k], dev(dr=1))

    peer_sq = sq.at[SIDE + z]
    for d in (1, 2, 3):
        send(own_sq, own_sq, sq_s, sq_r, dev(dz=d))
        send(own_sq, peer_sq, sq_s, sq_r, dev(dr=1, dz=d))
    send(own_sq, peer_sq, sq_s, sq_r, dev(dr=1))
    gather_send(0)
    for b in range(SIDE):
        cols = pl.ds(b * 512, 512)
        send(tok_hbm.at[:, cols], tok_peer.at[:, cols], tp_s, tp_r.at[b], dev(dr=1))
    gather_send(1)
    gather_send(2)
    send(w_hbm, w_peer, wp_s, wp_r, dev(dr=1))

    gain_load.wait()
    gain_row[...] = gain_flat[...].astype(F32).reshape(1, FEATS)

    arrived(sq.at[pl.ds(0, 7)], sq_r)
    for side in range(2):
        total = sq[4 * side] + sq[4 * side + 1] + sq[4 * side + 2] + sq[4 * side + 3]
        inv_row[:, pl.ds(side * ROWS, ROWS)] = lax.rsqrt(total * (1.0 / D) + 1e-05)

    def as_column(row):
        return jnp.broadcast_to(row[0:1], (128, ROWS)).T

    def product(k):
        first, count = CHUNKS[k]
        width, cq = count * 128, count * 32
        for c in range(count):
            for s in range(SIDE):
                toks = pl.ds(s * QUARTER, QUARTER)
                g = grads[first + c, toks, :].T.astype(F32)
                scaled_t[pl.ds(c * 128, 128), toks] = (g * inv_row[0:1, toks]).astype(BF16)

        def block(b):
            feats = pl.ds(b * 512, 512) if isinstance(b, int) else pl.ds(pl.multiple_of(b * 512, 512), 512)
            res = dot(scaled_t[pl.ds(0, width), pl.ds(0, ROWS)], tok[:, feats], (1, 0))
            res += dot(scaled_t[pl.ds(0, width), pl.ds(ROWS, ROWS)], tok_peer[:, feats], (1, 0))
            res = res.astype(BF16)
            for j in range(SIDE):
                for h in range(2):
                    for u in range(2):
                        lo = (2 * h + u) * cq
                        piece = res[lo : lo + cq, j * 128 : j * 128 + 128]
                        if h == 0:
                            part[k][h, j, u, b] = piece
                        else:
                            part[k][h, b, u, j] = piece

        if k == 0:
            for b in range(SIDE):
                arrived(tok_peer.at[:, pl.ds(b * 512, 512)], tp_r.at[b])
                block(b)
        else:
            pl.loop(0, SIDE)(block)

    def axis(h, stage):
        if (h == 0) == (stage == 0):
            return x, (lambda d: dev(dx=d))
        return y, (lambda d: dev(dy=d))

    def buffers(stage):
        return (part, got1a, got1b) if stage == 0 else (mid, got2a, got2b)

    def reduce_start(k, stage):
        src, got_a, got_b = buffers(stage)
        ss, rs = rs_s.at[k, stage], rs_r.at[k, stage]
        for h in range(2):
            m, to = axis(h, stage)
            far, up, down = (m + 2) % SIDE, (m + 1) % SIDE, (m + 3) % SIDE
            if STRAIGHT[k][stage]:
                send(src[k].at[h, far], got_b[k].at[h, 1], ss, rs.at[0], to(2))
                send(src[k].at[h, up], got_b[k].at[h, 0], ss, rs.at[0], to(1))
                send(src[k].at[h, down], got_b[k].at[h, 2], ss, rs.at[0], to(3))
                continue
            send(src[k].at[h, far, 0], got_a[k].at[h, 0], ss, rs.at[1], to(1))
            send(src[k].at[h, far, 1], got_a[k].at[h, 1], ss, rs.at[1], to(3))
            send(src[k].at[h, up, 1], got_b[k].at[h, 0, 1], ss, rs.at[0], to(1))
            send(src[k].at[h, down, 0], got_b[k].at[h, 1, 0], ss, rs.at[0], to(3))

    def add(a, b):
        return (a.astype(F32) + b.astype(F32)).astype(BF16)

    def reduce_pass(k, stage):
        if STRAIGHT[k][stage]:
            return
        src, got_a, got_b = buffers(stage)
        ss, rs = rs_s.at[k, stage], rs_r.at[k, stage]
        arrived(got_a[k], rs.at[1])
        for h in range(2):
            m, to = axis(h, stage)
            up, down = (m + 1) % SIDE, (m + 3) % SIDE
            src[k][h, up, 0] = add(src[k][h, up, 0], got_a[k][h, 0])
            send(src[k].at[h, up, 0], got_b[k].at[h, 0, 0], ss, rs.at[0], to(1))
            src[k][h, down, 1] = add(src[k][h, down, 1], got_a[k][h, 1])
            send(src[k].at[h, down, 1], got_b[k].at[h, 1, 1], ss, rs.at[0], to(3))

    def reduce_end(k, stage):
        src, _, got_b = buffers(stage)
        cq = CHUNKS[k][1] * 32
        arrived(got_b[k], rs_r.at[k, stage, 0])
        for h in range(2):
            m, _ = axis(h, stage)
            for u in range(2):
                total = src[k][h, m, u].astype(F32)
                for d in range(3 if STRAIGHT[k][stage] else 2):
                    total += got_b[k][h, d, u].astype(F32)
                if stage == 0:
                    for t in range(SIDE):
                        mid[k][h, t, u] = total[t].astype(BF16)
                else:
                    dw_t[pl.ds((2 * h + u) * cq, cq), :] = total

    def finish(k):
        first, count = CHUNKS[k]
        own = gain_row[0:1, pl.ds(pl.multiple_of(dp * 128, 128), 128)] * float(TOKENS) ** (-0.5)
        dw_ref[:, pl.ds(first * 128, count * 128)] = (dw_t[pl.ds(0, count * 128), :] * own).T.astype(BF16)

    def normed_grad(p):
        (own_lo, own_hi), (peer_lo, peer_hi) = PARTS[p]
        for k in range(N):
            if peer_lo <= CHUNKS[k][0] < peer_hi:
                arrived(other.at[slabs(k)], ot_r.at[k])
        if p == 0:
            w_load.wait()
            arrived(w_peer, wp_r)

        @pl.loop(0, SIDE)
        def _(b):
            feats = pl.ds(pl.multiple_of(b * 512, 512), 512)
            own = jnp.concatenate([grads[c, pl.ds(0, ROWS), :] for c in range(own_lo, own_hi)], axis=1)
            res = dot(own, w[feats, pl.ds(own_lo * 128, (own_hi - own_lo) * 128)], (1, 1))
            peer = jnp.concatenate([other[c] for c in range(peer_lo, peer_hi)], axis=1)
            res += dot(peer, w_peer[feats, pl.ds(peer_lo * 128, (peer_hi - peer_lo) * 128)], (1, 1))
            if p == 0:
                dn[:, feats] = res
            else:
                dn[:, feats] += res

    def inner_start():
        inv_col[...] = as_column(inv_row[:, 0:ROWS])
        dg_acc[...] = jnp.zeros_like(dg_acc)

        @pl.loop(0, ROWS // 16)
        def _(i):
            rows = pl.ds(pl.multiple_of(i * 16, 16), 16)
            inv = inv_col[rows, :]
            acc = jnp.zeros((16, 128), F32)
            for j in range(FEATS // 128):
                cols = pl.ds(j * 128, 128)
                prod = dn[rows, cols] * tok[rows, cols].astype(F32)
                acc += prod * gain_row[0:1, cols]
                prod = prod * inv
                dg_acc[:, cols] += prod[0:8] + prod[8:16]
            lanes[rows, :] = acc

        own_inner = inner_buf.at[z]
        own_inner[...] = lane_sums()
        for d in (1, 2, 3):
            send(own_inner, own_inner, in_s, in_r, dev(dz=d))
        own_dg = dg_a.at[r * SIDE + x]
        for j in range(FEATS // 128):
            own_dg[pl.ds(j, 1), :] = jnp.sum(dg_acc[:, pl.ds(j * 128, 128)], axis=0, keepdims=True)
        for d in (1, 2, 3):
            send(own_dg, own_dg, ga_s, ga_r, dev(dx=d))
            send(own_dg, own_dg, ga_s, ga_r, dev(dr=1, dx=d))
        send(own_dg, own_dg, ga_s, ga_r, dev(dr=1))

    def gain_y():
        arrived(dg_a.at[pl.ds(0, 7)], ga_r)
        total = dg_a[0]
        for i in range(1, 8):
            total += dg_a[i]
        own_dg = dg_b.at[y]
        own_dg[...] = total
        for d in (1, 2, 3):
            send(own_dg, own_dg, gb_s, gb_r, dev(dy=d))

    def gain_end():
        arrived(dg_b.at[pl.ds(0, 3)], gb_r)
        dgain_ref[...] = (dg_b[0] + dg_b[1] + dg_b[2] + dg_b[3]) * float(TOKENS) ** (-0.5)

    def tokens_end():
        arrived(inner_buf.at[pl.ds(0, 3)], in_r)
        inner = inner_buf[0] + inner_buf[1] + inner_buf[2] + inner_buf[3]
        inv = inv_row[:, 0:ROWS]
        log_scale = inner * inv * float(D) ** (-0.5)
        for j in range(SIDE):
            dlog_ref[pl.ds(j, 1), :] = log_scale[0:1, j * 128 : j * 128 + 128]
        coef_col[...] = as_column(inv * inv * inv * inner * (1.0 / D))
        res_load.wait()

        @pl.loop(0, ROWS // 16)
        def _(i):
            rows = pl.ds(pl.multiple_of(i * 16, 16), 16)
            inv_c, coef = inv_col[rows, :], coef_col[rows, :]
            for j in range(FEATS // 128):
                cols = pl.ds(j * 128, 128)
                scaled = dn[rows, cols] * gain_row[0:1, cols]
                value = dres[rows, cols].astype(F32) + inv_c * scaled
                dtok_ref[rows, cols] = (value - tok[rows, cols].astype(F32) * coef).astype(BF16)

    def step(k, n):
        if n == 0:
            gather_wait(k)
            product(k)
            reduce_start(k, 0)
        if n == 1:
            reduce_pass(k, 0)
        if n == 2:
            reduce_end(k, 0)
            reduce_start(k, 1)
        if n == 3:
            reduce_pass(k, 1)
        if n == 4:
            reduce_end(k, 1)
            finish(k)

    for i in range(N + 4):
        if 1 <= i and i + 1 < N:
            gather_relay(i + 1)
            if i + 2 < N:
                gather_send(i + 2)
        if i == N:
            normed_grad(1)
            inner_start()
        if i < N:
            step(i, 0)
        if i == 0:
            gather_relay(1)
        for n in range(1, 5):
            if 0 <= i - n < N:
                step(i - n, n)
        if i == 4:
            normed_grad(0)
        if i == N + 1:
            gain_y()
            tokens_end()
    gain_end()
    left(grads.at[pl.ds(0, 6)], ag_s)
    left(tok_peer, tp_s)
    left(w_peer, wp_s)
    left(other, ot_s)
    left(sq.at[pl.ds(0, 7)], sq_s)
    left(inner_buf.at[pl.ds(0, 3)], in_s)
    left(dg_a.at[pl.ds(0, 7)], ga_s)
    left(dg_b.at[pl.ds(0, 3)], gb_s)
    for k in range(N):
        left(part[k].at[:, pl.ds(0, 3)], rs_s.at[k, 0])
        left(mid[k].at[:, pl.ds(0, 3)], rs_s.at[k, 1])


def write_out(dtok, dw, dgain, dlog, dtok_hbm, dw_hbm, dgain_hbm, dlog_hbm, sem):
    pairs = ((dtok, dtok_hbm), (dw, dw_hbm), (dgain, dgain_hbm), (dlog, dlog_hbm))
    copies = [pltpu.make_async_copy(src, dst, sem.at[i]) for i, (src, dst) in enumerate(pairs)]
    for c in copies:
        c.start()
    for c in copies:
        c.wait()


def local(tokens, gain, weight, d_out, d_residual):
    vmem, dma = pltpu.VMEM, pltpu.SemaphoreType.DMA
    cqs = [count * 32 for _, count in CHUNKS]
    scratch = [
        vmem((ROWS, FEATS), BF16),
        vmem((ROWS, FEATS), BF16),
        vmem((SLABS, 2 * ROWS, 128), BF16),
        vmem((SLABS, ROWS, 128), BF16),
        vmem((FEATS, COLS), BF16),
        vmem((FEATS, COLS), BF16),
        vmem((ROWS, FEATS), F32),
        vmem((ROWS, FEATS), BF16),
        vmem((256, 2 * ROWS), BF16),
        vmem((FEATS,), BF16),
        vmem((1, FEATS), F32),
        vmem((ROWS, 128), F32),
        vmem((2 * SIDE, 8, ROWS), F32),
        vmem((8, 2 * ROWS), F32),
        vmem((ROWS, 128), F32),
        vmem((ROWS, 128), F32),
        vmem((SIDE, 8, ROWS), F32),
        vmem((8, FEATS), F32),
        vmem((2 * SIDE, 16, 128), F32),
        vmem((SIDE, 16, 128), F32),
        vmem((256, 128), F32),
    ]
    scratch += [vmem((2, SIDE, 2, SIDE, c, 128), BF16) for c in cqs]
    scratch += [vmem((2, 2, SIDE, c, 128), BF16) for c in cqs]
    scratch += [vmem((2, 2 + s[0], 2, SIDE, c, 128), BF16) for c, s in zip(cqs, STRAIGHT)]
    scratch += [vmem((2, SIDE, 2, c, 128), BF16) for c in cqs]
    scratch += [vmem((2, 2, c, 128), BF16) for c in cqs]
    scratch += [vmem((2, 2 + s[1], 2, c, 128), BF16) for c, s in zip(cqs, STRAIGHT)]
    scratch += [
        dma((5,)),
        dma,
        dma((N, 2)),
        dma,
        dma((SIDE,)),
        dma,
        dma,
        dma,
        dma((N,)),
        dma,
        dma,
        dma,
        dma,
        dma,
        dma,
        dma,
        dma,
        dma((N, 2)),
        dma((N, 2, 2)),
    ]
    hbm, in_vmem = pl.BlockSpec(memory_space=pltpu.HBM), pl.BlockSpec(memory_space=pltpu.VMEM)
    shapes = (((ROWS, FEATS), BF16), ((128, COLS), BF16), ((16, 128), F32), ((4, 128), F32))
    results = pl.pallas_call(
        kernel,
        name="fused",
        out_shape=tuple(pltpu.VMEM(*shape) for shape in shapes),
        in_specs=[hbm] * 5,
        out_specs=(in_vmem,) * 4,
        scratch_shapes=scratch,
        compiler_params=pltpu.CompilerParams(
            collective_id=0, has_side_effects=True, vmem_limit_bytes=48 * 2**20
        ),
        cost_estimate=pl.CostEstimate(flops=8 * 2**30, bytes_accessed=12 * 2**20, transcendentals=0),
    )(*[pltpu.with_memory_space_constraint(a, pltpu.HBM) for a in (tokens, gain, weight, d_out, d_residual)])
    d_tokens, d_weight, d_gain, d_log = pl.pallas_call(
        write_out,
        name="write_out",
        out_shape=tuple(jax.ShapeDtypeStruct(*shape) for shape in shapes),
        in_specs=[in_vmem] * 4,
        out_specs=(hbm,) * 4,
        scratch_shapes=[dma((4,))],
        compiler_params=pltpu.CompilerParams(vmem_limit_bytes=2**20),
    )(*results)
    return d_tokens, d_weight, d_gain.reshape(FEATS), d_log.reshape(ROWS)


def solution(mesh):
    in_specs = (
        P(("dp", "row"), "col"),
        P("col"),
        P("col", "row"),
        P(("dp", "col"), "row"),
        P(("dp", "row"), "col"),
    )
    out_specs = (P(("dp", "row"), "col"), P(("col", "dp"), "row"), P("col"), P(("dp", "row")))
    return jax.shard_map(local, mesh=mesh, in_specs=in_specs, out_specs=out_specs, check_vma=False)
```

time: 73 us -> 58.5 us (0.80)
  Pallas kernels: 65.8 us -> 57.8 us
  local copies, waits for them, and re-layouts: 6.38 us -> 0 us
    pallas_call x1 -> x2, Pallas kernels: 65.8 us -> 57.8 us  [the longest x1 56.3 us: local(): pl.pallas_call(kernel, name='fused', out_shape=tuple((pltpu.VMEM(*shape)...]
    unnamed x10 -> x0, local copies, waits for them, and re-layouts: 5.09 us -> none
    reshape x1 -> x0, local copies, waits for them, and re-layouts: 1.29 us -> none  [local(): gain.reshape(1, FEATS)]
where the time goes in v2:
time: 58.5 us; the launch traced here: 58.4 us
  Pallas kernels  57.8 us (99%)
  between operations  0.64 us (1%)
    pallas_call x1, Pallas kernels, local(): pl.pallas_call(kernel, name='fused', out_shape=tuple((pltpu.VMEM(*shape)...  56.3 us
    pallas_call x1, Pallas kernels, local(): pl.pallas_call(write_out, name='write_out', out_shape=tuple((jax.ShapeDty...  1.43 us

profile of v2, /device:TPU:0, one launch (start us, length us, event | category | flops | bytes accessed | tf_op | source)
XLA Modules:
  0.0 58.4 jit_solution(12981197891619499010)
XLA Ops:
  0.6 56.3 %fused.1 = (bf16[512,2048]{1,0:T(8,128)(2,1)S(1)}, bf16[128,1024]{1,0:T(8,128)(2,1)S(1)}, f32[16,128]{1,0:T(8,128)S(1)}, f32[4,128]{1,0:T(4,128)S(1)}) custom-call(bf16[512,2048]{1,0:T(8,128)(2,1)} %refs_0_.1, bf16[2048]{0:T(1024)(128)(2,1)} %refs_1_.1, bf16[2048,1024]{1,0:T(8,128)(2,1)} %refs_2_.1, bf16[256,1024]{1,0:T(8,128)(2,1)} %refs_3_.1, ...), custom_call_target="tpu_custom_call" | custom-call | flops 8589934592 | bytes 12582912 | tf_op jit(solution)/shard_map/fused/pallas_call | solution.py:446
  57.0 1.4 %write_out.1 = (bf16[512,2048]{1,0:T(8,128)(2,1)}, bf16[128,1024]{1,0:T(8,128)(2,1)}, f32[16,128]{1,0:T(8,128)}, f32[4,128]{1,0:T(4,128)}) custom-call(bf16[512,2048]{1,0:T(8,128)(2,1)S(1)} %get-tuple-element.12.dtok, bf16[128,1024]{1,0:T(8,128)(2,1)S(1)} %get-tuple-element.13.dw, f32[16,128]{1,0:T(8,128)S(1)} %get-tuple-element.14.dgain, ...), custom_call_target="tpu_custom_call" | custom-call | tf_op jit(solution)/shard_map/write_out/pallas_call | solution.py:458

commit v3 on v2

--- a/solution.py
+++ b/solution.py
@@ -15,10 +15,16 @@
 QUARTER = 256
 SIDE = 4
 SLABS = 8
-CHUNKS = ((0, 1), (1, 1), (2, 2), (4, 2), (6, 1), (7, 1))
+CHUNKS = ((0, 1), (1, 1), (2, 2), (4, 2), (6, 2))
 N = len(CHUNKS)
-STRAIGHT = ((0, 0), (0, 0), (0, 0), (0, 0), (0, 1), (1, 1))
+AHEAD = 3
+LEAD = 2
+STRAIGHT = ((0, 0), (0, 0), (0, 0), (0, 1), (1, 1))
+ORDER = (
+    ("M", 0), ("M", 1), ("P", 0), ("M", 2), ("P", 1), ("E", 0), ("normed", 0), ("M", 3), ("P", 2), ("E", 1), ("Q", 0), ("M", 4), ("normed", 1), ("P", 3), ("E", 2), ("Q", 1), ("F", 0), ("inner", 0), ("E", 3), ("E", 4), ("Q", 2), ("F", 1), ("gain", 0), ("F", 2), ("tokens", 0), ("F", 3), ("F", 4),
+)
 PARTS = (((0, 4), (0, 4)), ((4, 8), (4, 8)))
+FIRST_PEER = 0
 
 
 def dot(a, b, dims):
@@ -80,12 +86,48 @@
     for partner in partners:
         pl.semaphore_signal(barrier, inc=1, device_id=partner, device_id_type=MESH)
 
-    tok_load = load(tok_hbm, tok, 0)
     for c in range(SLABS):
         load(dout_hbm.at[:, pl.ds(c * 128, 128)], grads.at[c, slot(z)], 1)
+    tok_load = load(tok_hbm, tok, 0)
     gain_load = load(gain_hbm, gain_flat, 2)
     w_load = load(w_hbm, w, 3)
     res_load = load(dres_hbm, dres, 4)
+
+    def gather_send(c):
+        own = grads.at[c, slot(z)]
+        for d in (1, 3) if c else (1, 3, 2):
+            send(own, own, ag_s, ag_r.at[c, 0], dev(dz=d))
+
+    relayed = [0]
+
+    def gather_relay(hi):
+        while relayed[0] < min(hi, SLABS - 1):
+            relayed[0] += 1
+            c = relayed[0]
+            arrived(grads.at[c, pl.ds(0, 2 * QUARTER)], ag_r.at[c, 0])
+            low, high = grads.at[c, half_slot(z + 1, 0)], grads.at[c, half_slot(z + 3, 1)]
+            send(low, low, ag_s, ag_r.at[c, 1], dev(dz=3))
+            send(high, high, ag_s, ag_r.at[c, 1], dev(dz=1))
+            if c + AHEAD < SLABS:
+                gather_send(c + AHEAD)
+
+    def gather_wait(k):
+        for c in range(CHUNKS[k][0], sum(CHUNKS[k])):
+            if c == 0:
+                arrived(grads.at[c, pl.ds(0, 3 * QUARTER)], ag_r.at[c, 0])
+            else:
+                gather_relay(c + LEAD)
+                arrived(grads.at[c, pl.ds(0, QUARTER)], ag_r.at[c, 1])
+        send(grads.at[slabs(k), pl.ds(ROWS, ROWS)], other.at[slabs(k)], ot_s, ot_r.at[k], dev(dr=1))
+
+    own_quarter = grads.at[:, slot(z)]
+    pltpu.make_async_copy(own_quarter, own_quarter, local_sem.at[1]).wait()
+    pl.semaphore_wait(barrier, len(partners))
+    gather_send(0)
+    for b in range(SIDE):
+        cols = pl.ds(b * 512, 512)
+        send(tok_hbm.at[:, cols], tok_peer.at[:, cols], tp_s, tp_r.at[b], dev(dr=1))
+    send(w_hbm, w_peer, wp_s, wp_r, dev(dr=1))
 
     tok_load.wait()
 
@@ -104,42 +146,13 @@
 
     own_sq = sq.at[z]
     own_sq[...] = lane_sums()
-    own_quarter = grads.at[:, slot(z)]
-    pltpu.make_async_copy(own_quarter, own_quarter, local_sem.at[1]).wait()
-    pl.semaphore_wait(barrier, len(partners))
-
-    def gather_send(k):
-        own = grads.at[slabs(k), slot(z)]
-        for d in (1, 3) if k else (1, 3, 2):
-            send(own, own, ag_s, ag_r.at[k, 0], dev(dz=d))
-
-    def gather_relay(k):
-        if k == 0:
-            return
-        arrived(grads.at[slabs(k), pl.ds(0, 2 * QUARTER)], ag_r.at[k, 0])
-        low, high = grads.at[slabs(k), half_slot(z + 1, 0)], grads.at[slabs(k), half_slot(z + 3, 1)]
-        send(low, low, ag_s, ag_r.at[k, 1], dev(dz=3))
-        send(high, high, ag_s, ag_r.at[k, 1], dev(dz=1))
-
-    def gather_wait(k):
-        if k == 0:
-            arrived(grads.at[slabs(k), pl.ds(0, 3 * QUARTER)], ag_r.at[k, 0])
-        else:
-            arrived(grads.at[slabs(k), pl.ds(0, QUARTER)], ag_r.at[k, 1])
-        send(grads.at[slabs(k), pl.ds(ROWS, ROWS)], other.at[slabs(k)], ot_s, ot_r.at[k], dev(dr=1))
-
     peer_sq = sq.at[SIDE + z]
     for d in (1, 2, 3):
         send(own_sq, own_sq, sq_s, sq_r, dev(dz=d))
         send(own_sq, peer_sq, sq_s, sq_r, dev(dr=1, dz=d))
     send(own_sq, peer_sq, sq_s, sq_r, dev(dr=1))
-    gather_send(0)
-    for b in range(SIDE):
-        cols = pl.ds(b * 512, 512)
-        send(tok_hbm.at[:, cols], tok_peer.at[:, cols], tp_s, tp_r.at[b], dev(dr=1))
-    gather_send(1)
-    gather_send(2)
-    send(w_hbm, w_peer, wp_s, wp_r, dev(dr=1))
+    for c in range(1, AHEAD + 1):
+        gather_send(c)
 
     gain_load.wait()
     gain_row[...] = gain_flat[...].astype(F32).reshape(1, FEATS)
@@ -180,6 +193,8 @@
             for b in range(SIDE):
                 arrived(tok_peer.at[:, pl.ds(b * 512, 512)], tp_r.at[b])
                 block(b)
+                if b > 0:
+                    gather_relay(b)
         else:
             pl.loop(0, SIDE)(block)
 
@@ -246,21 +261,26 @@
         dw_ref[:, pl.ds(first * 128, count * 128)] = (dw_t[pl.ds(0, count * 128), :] * own).T.astype(BF16)
 
     def normed_grad(p):
-        (own_lo, own_hi), (peer_lo, peer_hi) = PARTS[p]
-        for k in range(N):
-            if peer_lo <= CHUNKS[k][0] < peer_hi:
-                arrived(other.at[slabs(k)], ot_r.at[k])
+        sources = [(grads, w, PARTS[p][0]), (other, w_peer, PARTS[p][1])]
+        if PARTS[p][1]:
+            for k in range(N):
+                if CHUNKS[k][0] in range(*PARTS[p][1]):
+                    arrived(other.at[slabs(k)], ot_r.at[k])
         if p == 0:
             w_load.wait()
+        if p == FIRST_PEER:
             arrived(w_peer, wp_r)
 
         @pl.loop(0, SIDE)
         def _(b):
             feats = pl.ds(pl.multiple_of(b * 512, 512), 512)
-            own = jnp.concatenate([grads[c, pl.ds(0, ROWS), :] for c in range(own_lo, own_hi)], axis=1)
-            res = dot(own, w[feats, pl.ds(own_lo * 128, (own_hi - own_lo) * 128)], (1, 1))
-            peer = jnp.concatenate([other[c] for c in range(peer_lo, peer_hi)], axis=1)
-            res += dot(peer, w_peer[feats, pl.ds(peer_lo * 128, (peer_hi - peer_lo) * 128)], (1, 1))
+            res = None
+            for rows, weights, span in sources:
+                if span:
+                    left_side = jnp.concatenate([rows[c, pl.ds(0, ROWS), :] for c in range(*span)], axis=1)
+                    right_side = weights[feats, pl.ds(span[0] * 128, (span[1] - span[0]) * 128)]
+                    term = dot(left_side, right_side, (1, 1))
+                    res = term if res is None else res + term
             if p == 0:
                 dn[:, feats] = res
             else:
@@ -334,6 +354,7 @@
             gather_wait(k)
             product(k)
             reduce_start(k, 0)
+            gather_relay(sum(CHUNKS[k]) + LEAD)
         if n == 1:
             reduce_pass(k, 0)
         if n == 2:
@@ -345,26 +366,17 @@
             reduce_end(k, 1)
             finish(k)
 
-    for i in range(N + 4):
-        if 1 <= i and i + 1 < N:
-            gather_relay(i + 1)
-            if i + 2 < N:
-                gather_send(i + 2)
-        if i == N:
-            normed_grad(1)
+    for what, k in ORDER:
+        if what == "normed":
+            normed_grad(k)
+        elif what == "inner":
             inner_start()
-        if i < N:
-            step(i, 0)
-        if i == 0:
-            gather_relay(1)
-        for n in range(1, 5):
-            if 0 <= i - n < N:
-                step(i - n, n)
-        if i == 4:
-            normed_grad(0)
-        if i == N + 1:
+        elif what == "tokens":
+            tokens_end()
+        elif what == "gain":
             gain_y()
-            tokens_end()
+        else:
+            step(k, "MPEQF".index(what))
     gain_end()
     left(grads.at[pl.ds(0, 6)], ag_s)
     left(tok_peer, tp_s)
@@ -423,7 +435,7 @@
     scratch += [
         dma((5,)),
         dma,
-        dma((N, 2)),
+        dma((SLABS, 2)),
         dma,
         dma((SIDE,)),
         dma,

time: 58.5 us -> 54.9 us (0.938)
  Pallas kernels: 57.8 us -> 54.1 us
    pallas_call x1, Pallas kernels: 56.3 us -> 52.7 us  [local(): pl.pallas_call(kernel, name='fused', out_shape=tuple((pltpu.VMEM(*shape)...]
where the time goes in v3:
time: 54.9 us; the launch traced here: 54.8 us
  Pallas kernels  54.1 us (99%)
  between operations  0.64 us (1%)
    pallas_call x1, Pallas kernels, local(): pl.pallas_call(kernel, name='fused', out_shape=tuple((pltpu.VMEM(*shape)...  52.7 us
    pallas_call x1, Pallas kernels, local(): pl.pallas_call(write_out, name='write_out', out_shape=tuple((jax.ShapeDty...  1.43 us

profile of v3, /device:TPU:0, one launch (start us, length us, event | category | flops | bytes accessed | tf_op | source)
XLA Modules:
  0.0 54.8 jit_solution(9936623235707365849)
XLA Ops:
  0.6 52.7 %fused.1 = (bf16[512,2048]{1,0:T(8,128)(2,1)S(1)}, bf16[128,1024]{1,0:T(8,128)(2,1)S(1)}, f32[16,128]{1,0:T(8,128)S(1)}, f32[4,128]{1,0:T(4,128)S(1)}) custom-call(bf16[512,2048]{1,0:T(8,128)(2,1)} %refs_0_.1, bf16[2048]{0:T(1024)(128)(2,1)} %refs_1_.1, bf16[2048,1024]{1,0:T(8,128)(2,1)} %refs_2_.1, bf16[256,1024]{1,0:T(8,128)(2,1)} %refs_3_.1, ...), custom_call_target="tpu_custom_call" | custom-call | flops 8589934592 | bytes 12582912 | tf_op jit(solution)/shard_map/fused/pallas_call | solution.py:458
  53.3 1.4 %write_out.1 = (bf16[512,2048]{1,0:T(8,128)(2,1)}, bf16[128,1024]{1,0:T(8,128)(2,1)}, f32[16,128]{1,0:T(8,128)}, f32[4,128]{1,0:T(4,128)}) custom-call(bf16[512,2048]{1,0:T(8,128)(2,1)S(1)} %get-tuple-element.12.dtok, bf16[128,1024]{1,0:T(8,128)(2,1)S(1)} %get-tuple-element.13.dw, f32[16,128]{1,0:T(8,128)S(1)} %get-tuple-element.14.dgain, ...), custom_call_target="tpu_custom_call" | custom-call | tf_op jit(solution)/shard_map/write_out/pallas_call | solution.py:470

commit v4 on v3

--- a/solution.py
+++ b/solution.py
@@ -21,7 +21,7 @@
 LEAD = 2
 STRAIGHT = ((0, 0), (0, 0), (0, 0), (0, 1), (1, 1))
 ORDER = (
-    ("M", 0), ("M", 1), ("P", 0), ("M", 2), ("P", 1), ("E", 0), ("normed", 0), ("M", 3), ("P", 2), ("E", 1), ("Q", 0), ("M", 4), ("normed", 1), ("P", 3), ("E", 2), ("Q", 1), ("F", 0), ("inner", 0), ("E", 3), ("E", 4), ("Q", 2), ("F", 1), ("gain", 0), ("F", 2), ("tokens", 0), ("F", 3), ("F", 4),
+    ("M", 0), ("M", 1), ("P", 0), ("M", 2), ("P", 1), ("E", 0), ("normed", 0), ("M", 3), ("P", 2), ("E", 1), ("Q", 0), ("M", 4), ("normed", 1), ("inner", 0), ("P", 3), ("E", 2), ("Q", 1), ("F", 0), ("E", 3), ("E", 4), ("Q", 2), ("F", 1), ("gain", 0), ("tokens", 0), ("F", 2), ("F", 3), ("F", 4),
 )
 PARTS = (((0, 4), (0, 4)), ((4, 8), (4, 8)))
 FIRST_PEER = 0

time: 54.9 us -> 53.6 us (0.976)
  Pallas kernels: 54.1 us -> 52.9 us
    pallas_call x1, Pallas kernels: 52.7 us -> 51.4 us  [local(): pl.pallas_call(kernel, name='fused', out_shape=tuple((pltpu.VMEM(*shape)...]
where the time goes in v4:
time: 53.6 us; the launch traced here: 53.5 us
  Pallas kernels  52.9 us (99%)
  between operations  0.64 us (1%)
    pallas_call x1, Pallas kernels, local(): pl.pallas_call(kernel, name='fused', out_shape=tuple((pltpu.VMEM(*shape)...  51.4 us
    pallas_call x1, Pallas kernels, local(): pl.pallas_call(write_out, name='write_out', out_shape=tuple((jax.ShapeDty...  1.43 us

profile of v4, /device:TPU:0, one launch (start us, length us, event | category | flops | bytes accessed | tf_op | source)
XLA Modules:
  0.0 53.5 jit_solution(5358245608016581411)
XLA Ops:
  0.6 51.4 %fused.1 = (bf16[512,2048]{1,0:T(8,128)(2,1)S(1)}, bf16[128,1024]{1,0:T(8,128)(2,1)S(1)}, f32[16,128]{1,0:T(8,128)S(1)}, f32[4,128]{1,0:T(4,128)S(1)}) custom-call(bf16[512,2048]{1,0:T(8,128)(2,1)} %refs_0_.1, bf16[2048]{0:T(1024)(128)(2,1)} %refs_1_.1, bf16[2048,1024]{1,0:T(8,128)(2,1)} %refs_2_.1, bf16[256,1024]{1,0:T(8,128)(2,1)} %refs_3_.1, ...), custom_call_target="tpu_custom_call" | custom-call | flops 8589934592 | bytes 12582912 | tf_op jit(solution)/shard_map/fused/pallas_call | solution.py:458
  52.1 1.4 %write_out.1 = (bf16[512,2048]{1,0:T(8,128)(2,1)}, bf16[128,1024]{1,0:T(8,128)(2,1)}, f32[16,128]{1,0:T(8,128)}, f32[4,128]{1,0:T(4,128)}) custom-call(bf16[512,2048]{1,0:T(8,128)(2,1)S(1)} %get-tuple-element.12.dtok, bf16[128,1024]{1,0:T(8,128)(2,1)S(1)} %get-tuple-element.13.dw, f32[16,128]{1,0:T(8,128)S(1)} %get-tuple-element.14.dgain, ...), custom_call_target="tpu_custom_call" | custom-call | tf_op jit(solution)/shard_map/write_out/pallas_call | solution.py:470

commit v5 on v4

--- a/solution.py
+++ b/solution.py
@@ -18,10 +18,10 @@
 CHUNKS = ((0, 1), (1, 1), (2, 2), (4, 2), (6, 2))
 N = len(CHUNKS)
 AHEAD = 3
-LEAD = 2
+LEAD = 1
 STRAIGHT = ((0, 0), (0, 0), (0, 0), (0, 1), (1, 1))
 ORDER = (
-    ("M", 0), ("M", 1), ("P", 0), ("M", 2), ("P", 1), ("E", 0), ("normed", 0), ("M", 3), ("P", 2), ("E", 1), ("Q", 0), ("M", 4), ("normed", 1), ("inner", 0), ("P", 3), ("E", 2), ("Q", 1), ("F", 0), ("E", 3), ("E", 4), ("Q", 2), ("F", 1), ("gain", 0), ("tokens", 0), ("F", 2), ("F", 3), ("F", 4),
+    ("M", 0), ("S", 0), ("M", 1), ("P", 0), ("S", 1), ("M", 2), ("P", 1), ("E", 0), ("S", 2), ("M", 3), ("P", 2), ("E", 1), ("Q", 0), ("S", 3), ("normed", 0), ("M", 4), ("S", 4), ("P", 3), ("normed", 1), ("inner", 0), ("E", 2), ("Q", 1), ("F", 0), ("E", 3), ("E", 4), ("Q", 2), ("F", 1), ("gain", 0), ("tokens", 0), ("F", 2), ("F", 3), ("F", 4),
 )
 PARTS = (((0, 4), (0, 4)), ((4, 8), (4, 8)))
 FIRST_PEER = 0
@@ -35,7 +35,8 @@
     it = iter(refs)
     tok_hbm, gain_hbm, w_hbm, dout_hbm, dres_hbm = [next(it) for _ in range(5)]
     dtok_ref, dw_ref, dgain_ref, dlog_ref = [next(it) for _ in range(4)]
-    tok, tok_peer, grads, other, w, w_peer, dn, dres, scaled_t = [next(it) for _ in range(9)]
+    toks_both, grads, other, w, w_peer, dn, dres, scaled_t = [next(it) for _ in range(8)]
+    tok, tok_peer = toks_both.at[pl.ds(0, ROWS)], toks_both.at[pl.ds(ROWS, ROWS)]
     gain_flat, gain_row, lanes, sq, inv_row, inv_col, coef_col, inner_buf = [next(it) for _ in range(8)]
     dg_acc, dg_a, dg_b, dw_t = [next(it) for _ in range(4)]
     part, got1a, got1b, mid, got2a, got2b = [[next(it) for _ in range(N)] for _ in range(6)]
@@ -124,10 +125,9 @@
     pltpu.make_async_copy(own_quarter, own_quarter, local_sem.at[1]).wait()
     pl.semaphore_wait(barrier, len(partners))
     gather_send(0)
-    for b in range(SIDE):
+    for b in range(0, 2):
         cols = pl.ds(b * 512, 512)
         send(tok_hbm.at[:, cols], tok_peer.at[:, cols], tp_s, tp_r.at[b], dev(dr=1))
-    send(w_hbm, w_peer, wp_s, wp_r, dev(dr=1))
 
     tok_load.wait()
 
@@ -153,6 +153,10 @@
     send(own_sq, peer_sq, sq_s, sq_r, dev(dr=1))
     for c in range(1, AHEAD + 1):
         gather_send(c)
+    for b in range(2, 4):
+        cols = pl.ds(b * 512, 512)
+        send(tok_hbm.at[:, cols], tok_peer.at[:, cols], tp_s, tp_r.at[b], dev(dr=1))
+    send(w_hbm, w_peer, wp_s, wp_r, dev(dr=1))
 
     gain_load.wait()
     gain_row[...] = gain_flat[...].astype(F32).reshape(1, FEATS)
@@ -176,9 +180,7 @@
 
         def block(b):
             feats = pl.ds(b * 512, 512) if isinstance(b, int) else pl.ds(pl.multiple_of(b * 512, 512), 512)
-            res = dot(scaled_t[pl.ds(0, width), pl.ds(0, ROWS)], tok[:, feats], (1, 0))
-            res += dot(scaled_t[pl.ds(0, width), pl.ds(ROWS, ROWS)], tok_peer[:, feats], (1, 0))
-            res = res.astype(BF16)
+            res = dot(scaled_t[pl.ds(0, width), :], toks_both[:, feats], (1, 0)).astype(BF16)
             for j in range(SIDE):
                 for h in range(2):
                     for u in range(2):
@@ -274,13 +276,12 @@
         @pl.loop(0, SIDE)
         def _(b):
             feats = pl.ds(pl.multiple_of(b * 512, 512), 512)
-            res = None
-            for rows, weights, span in sources:
+            rows, weights = [], []
+            for grad, weight, span in sources:
                 if span:
-                    left_side = jnp.concatenate([rows[c, pl.ds(0, ROWS), :] for c in range(*span)], axis=1)
-                    right_side = weights[feats, pl.ds(span[0] * 128, (span[1] - span[0]) * 128)]
-                    term = dot(left_side, right_side, (1, 1))
-                    res = term if res is None else res + term
+                    rows += [grad[c, pl.ds(0, ROWS), :] for c in range(*span)]
+                    weights.append(weight[feats, pl.ds(span[0] * 128, (span[1] - span[0]) * 128)])
+            res = dot(jnp.concatenate(rows, axis=1), jnp.concatenate(weights, axis=1), (1, 1))
             if p == 0:
                 dn[:, feats] = res
             else:
@@ -353,8 +354,9 @@
         if n == 0:
             gather_wait(k)
             product(k)
+            gather_relay(sum(CHUNKS[k]) + LEAD)
+        if n == 5:
             reduce_start(k, 0)
-            gather_relay(sum(CHUNKS[k]) + LEAD)
         if n == 1:
             reduce_pass(k, 0)
         if n == 2:
@@ -376,7 +378,7 @@
         elif what == "gain":
             gain_y()
         else:
-            step(k, "MPEQF".index(what))
+            step(k, "MPEQFS".index(what))
     gain_end()
     left(grads.at[pl.ds(0, 6)], ag_s)
     left(tok_peer, tp_s)
@@ -404,8 +406,7 @@
     vmem, dma = pltpu.VMEM, pltpu.SemaphoreType.DMA
     cqs = [count * 32 for _, count in CHUNKS]
     scratch = [
-        vmem((ROWS, FEATS), BF16),
-        vmem((ROWS, FEATS), BF16),
+        vmem((2 * ROWS, FEATS), BF16),
         vmem((SLABS, 2 * ROWS, 128), BF16),
         vmem((SLABS, ROWS, 128), BF16),
         vmem((FEATS, COLS), BF16),

time: 53.6 us -> 52.7 us (0.983)
  Pallas kernels: 52.9 us -> 52 us
    pallas_call x1, Pallas kernels: 51.4 us -> 50.5 us  [local(): pl.pallas_call(kernel, name='fused', out_shape=tuple((pltpu.VMEM(*shape)...]
where the time goes in v5:
time: 52.7 us; the launch traced here: 52.6 us
  Pallas kernels  52 us (99%)
  between operations  0.64 us (1%)
    pallas_call x1, Pallas kernels, local(): pl.pallas_call(kernel, name='fused', out_shape=tuple((pltpu.VMEM(*shape)...  50.5 us
    pallas_call x1, Pallas kernels, local(): pl.pallas_call(write_out, name='write_out', out_shape=tuple((jax.ShapeDty...  1.43 us

profile of v5, /device:TPU:0, one launch (start us, length us, event | category | flops | bytes accessed | tf_op | source)
XLA Modules:
  0.0 52.6 jit_solution(177388530046639897)
XLA Ops:
  0.6 50.5 %fused.1 = (bf16[512,2048]{1,0:T(8,128)(2,1)S(1)}, bf16[128,1024]{1,0:T(8,128)(2,1)S(1)}, f32[16,128]{1,0:T(8,128)S(1)}, f32[4,128]{1,0:T(4,128)S(1)}) custom-call(bf16[512,2048]{1,0:T(8,128)(2,1)} %refs_0_.1, bf16[2048]{0:T(1024)(128)(2,1)} %refs_1_.1, bf16[2048,1024]{1,0:T(8,128)(2,1)} %refs_2_.1, bf16[256,1024]{1,0:T(8,128)(2,1)} %refs_3_.1, ...), custom_call_target="tpu_custom_call" | custom-call | flops 8589934592 | bytes 12582912 | tf_op jit(solution)/shard_map/fused/pallas_call | solution.py:459
  51.2 1.4 %write_out.1 = (bf16[512,2048]{1,0:T(8,128)(2,1)}, bf16[128,1024]{1,0:T(8,128)(2,1)}, f32[16,128]{1,0:T(8,128)}, f32[4,128]{1,0:T(4,128)}) custom-call(bf16[512,2048]{1,0:T(8,128)(2,1)S(1)} %get-tuple-element.12.dtok, bf16[128,1024]{1,0:T(8,128)(2,1)S(1)} %get-tuple-element.13.dw, f32[16,128]{1,0:T(8,128)S(1)} %get-tuple-element.14.dgain, ...), custom_call_target="tpu_custom_call" | custom-call | tf_op jit(solution)/shard_map/write_out/pallas_call | solution.py:471

commit v6 on v5

--- a/solution.py
+++ b/solution.py
@@ -18,7 +18,7 @@
 CHUNKS = ((0, 1), (1, 1), (2, 2), (4, 2), (6, 2))
 N = len(CHUNKS)
 AHEAD = 3
-LEAD = 1
+LEAD = 2
 STRAIGHT = ((0, 0), (0, 0), (0, 0), (0, 1), (1, 1))
 ORDER = (
     ("M", 0), ("S", 0), ("M", 1), ("P", 0), ("S", 1), ("M", 2), ("P", 1), ("E", 0), ("S", 2), ("M", 3), ("P", 2), ("E", 1), ("Q", 0), ("S", 3), ("normed", 0), ("M", 4), ("S", 4), ("P", 3), ("normed", 1), ("inner", 0), ("E", 2), ("Q", 1), ("F", 0), ("E", 3), ("E", 4), ("Q", 2), ("F", 1), ("gain", 0), ("tokens", 0), ("F", 2), ("F", 3), ("F", 4),

time: 52.7 us -> 52 us (0.987)
  Pallas kernels: 52 us -> 51.2 us
    pallas_call x1, Pallas kernels: 50.5 us -> 49.8 us  [local(): pl.pallas_call(kernel, name='fused', out_shape=tuple((pltpu.VMEM(*shape)...]
where the time goes in v6:
time: 52 us; the launch traced here: 51.9 us
  Pallas kernels  51.2 us (98%)
  between operations  0.64 us (1%)
    pallas_call x1, Pallas kernels, local(): pl.pallas_call(kernel, name='fused', out_shape=tuple((pltpu.VMEM(*shape)...  49.8 us
    pallas_call x1, Pallas kernels, local(): pl.pallas_call(write_out, name='write_out', out_shape=tuple((jax.ShapeDty...  1.43 us

profile of v6, /device:TPU:0, one launch (start us, length us, event | category | flops | bytes accessed | tf_op | source)
XLA Modules:
  0.0 51.9 jit_solution(15450733744495037948)
XLA Ops:
  0.6 49.8 %fused.1 = (bf16[512,2048]{1,0:T(8,128)(2,1)S(1)}, bf16[128,1024]{1,0:T(8,128)(2,1)S(1)}, f32[16,128]{1,0:T(8,128)S(1)}, f32[4,128]{1,0:T(4,128)S(1)}) custom-call(bf16[512,2048]{1,0:T(8,128)(2,1)} %refs_0_.1, bf16[2048]{0:T(1024)(128)(2,1)} %refs_1_.1, bf16[2048,1024]{1,0:T(8,128)(2,1)} %refs_2_.1, bf16[256,1024]{1,0:T(8,128)(2,1)} %refs_3_.1, ...), custom_call_target="tpu_custom_call" | custom-call | flops 8589934592 | bytes 12582912 | tf_op jit(solution)/shard_map/fused/pallas_call | solution.py:459
  50.4 1.4 %write_out.1 = (bf16[512,2048]{1,0:T(8,128)(2,1)}, bf16[128,1024]{1,0:T(8,128)(2,1)}, f32[16,128]{1,0:T(8,128)}, f32[4,128]{1,0:T(4,128)}) custom-call(bf16[512,2048]{1,0:T(8,128)(2,1)S(1)} %get-tuple-element.12.dtok, bf16[128,1024]{1,0:T(8,128)(2,1)S(1)} %get-tuple-element.13.dw, f32[16,128]{1,0:T(8,128)S(1)} %get-tuple-element.14.dgain, ...), custom_call_target="tpu_custom_call" | custom-call | tf_op jit(solution)/shard_map/write_out/pallas_call | solution.py:471
